TPU v7x, 768 devices: a whole 4x8x12 slice. The times are simulated.
768 devices in a mesh: dp: 12 (over z), seq: 8 (over x, core), head: 8 (over y).
Axes of the slice: x: 4, y: 8, z: 12, core: 2. Of those that a mesh axis runs over, the one named last changes fastest.
Arguments:
- tokens: bfloat16 [98304, 1536], P(('dp', 'seq', 'head')), may hold values from -6 to 6
- norm_gain: float32 [1536], replicated, may hold values from 0.5 to 1.5
- w_up: bfloat16 [64, 1536, 1536], P(('seq', 'head')), may hold values from -0.15625 to 0.15625
- w_down: bfloat16 [64, 1536, 1536], P(('seq', 'head')), may hold values from -0.15625 to 0.15625
- routes: int32 [98304, 2], P(('dp', 'seq', 'head')), may hold values from 0 to 63, all different within a row; in each aligned block of 128 rows (0 to 127, 128 to 255, ...) at most 4 rows name the same one
- combine: float32 [98304, 2], P(('dp', 'seq', 'head')), may hold values from 0.1 to 1
- loss_mask: int32 [98304], P(('dp', 'seq', 'head')), may hold values from 0 to 1, as said below
Outputs:
- grad_tokens: bfloat16 [98304, 1536], P(('dp', 'seq', 'head'))
- grad_gain: float32 [1536], replicated
- grad_combine: float32 [98304, 2], P(('dp', 'seq', 'head'))
- loss_value: float32 [], replicated
Inputs may be any that keep to these rules, and one draw needn't show every extreme that they name: `routes`: the 2 experts of a token differ. Among the tokens of one device no expert is named more than 4 times; every expert is named somewhere. `loss_mask`: every eighth token (positions 7, 15, 23, ...) has 1.
All inputs are finite; a program needn't handle non-finite values.
Results may differ from a plain program's by a relative error of at most 0.0085.
Values may be sent and summed in bfloat16 or wider, within the bound.
A program may use at most 64 MiB of HBM per device.

v0:
```python
import jax
import jax.numpy as jnp
from jax import lax
from jax.sharding import PartitionSpec as P


def shuffle(row_block, peer_count, capacity):
    feature = row_block.shape[1]
    blocks = row_block.reshape(peer_count, capacity, feature)
    moved = lax.all_to_all(blocks, ("seq", "head"), split_axis=0, concat_axis=0, tiled=True)
    return moved.reshape(peer_count * capacity, feature)


def on_device(tokens, norm_gain, w_up, w_down, routes, combine, loss_mask):
    tok_rows, feature = tokens.shape
    top_count = routes.shape[1]
    peer_count = lax.axis_size(("seq", "head"))
    capacity = max(2, (tok_rows * top_count + peer_count - 1) // peer_count)
    all_devices = lax.axis_size(("dp", "seq", "head"))
    mask_f = loss_mask.astype(jnp.float32)
    count = lax.psum(jnp.sum(mask_f), ("dp", "seq", "head"))
    inputs = tokens.astype(jnp.float32)
    inverse = lax.rsqrt(jnp.mean(inputs * inputs, axis=-1, keepdims=True) + 1e-05)
    normed = inputs * inverse
    scaled = (normed * norm_gain).astype(jnp.bfloat16)
    flat_routes = routes.reshape(-1)
    onehot = (flat_routes[:, None] == jnp.arange(peer_count, dtype=jnp.int32)[None, :]).astype(
        jnp.int32
    )
    position = jnp.sum((jnp.cumsum(onehot, axis=0) - onehot) * onehot, axis=1)
    bucket = flat_routes * capacity + position
    placement = (
        jnp.arange(peer_count * capacity, dtype=jnp.int32)[:, None] == bucket[None, :]
    ).astype(jnp.bfloat16)
    token_place = jnp.sum(placement.reshape(peer_count * capacity, tok_rows, top_count), axis=2)
    send_rows = jnp.dot(token_place, scaled, preferred_element_type=jnp.float32).astype(
        jnp.bfloat16
    )
    arrived = shuffle(send_rows, peer_count, capacity)
    weight_up = w_up[0]
    weight_down = w_down[0]
    projected = jnp.dot(arrived, weight_up, preferred_element_type=jnp.float32)
    gate_value = jax.nn.sigmoid(1.702 * projected)
    hidden = (projected * gate_value).astype(jnp.bfloat16)
    expert_out = jnp.dot(hidden, weight_down, preferred_element_type=jnp.float32).astype(
        jnp.bfloat16
    )
    returned = shuffle(expert_out, peer_count, capacity)
    picked = returned[bucket].reshape(tok_rows, top_count, feature).astype(jnp.float32)
    mixed = inputs + jnp.sum(combine[:, :, None] * picked, axis=1)
    cotangent = mask_f[:, None] * mixed
    loss_part = jnp.sum(mask_f * jnp.sum(mixed * mixed, axis=-1))
    combine_part = jnp.sum(cotangent[:, None, :] * picked, axis=-1)
    scaled_cot = (
        (combine[:, :, None] * cotangent[:, None, :])
        .astype(jnp.bfloat16)
        .reshape(tok_rows * top_count, feature)
    )
    send_cot = jnp.dot(placement, scaled_cot, preferred_element_type=jnp.float32).astype(
        jnp.bfloat16
    )
    arrived_cot = shuffle(send_cot, peer_count, capacity)
    hidden_grad = lax.dot_general(
        arrived_cot, weight_down, (((1,), (1,)), ((), ())), preferred_element_type=jnp.float32
    )
    slope = gate_value + 1.702 * projected * gate_value * (1.0 - gate_value)
    pre_grad = (hidden_grad * slope).astype(jnp.bfloat16)
    row_grad = lax.dot_general(
        pre_grad, weight_up, (((1,), (1,)), ((), ())), preferred_element_type=jnp.float32
    ).astype(jnp.bfloat16)
    returned_grad = shuffle(row_grad, peer_count, capacity)
    normed_total = jnp.sum(
        returned_grad[bucket].reshape(tok_rows, top_count, feature).astype(jnp.float32), axis=1
    )
    gain_part = jnp.sum(normed_total * normed, axis=0)
    normed_grad = normed_total * norm_gain
    input_grad = inverse * (
        normed_grad - normed * jnp.mean(normed_grad * normed, axis=-1, keepdims=True)
    )
    gain_total, loss_total = lax.psum((gain_part, loss_part), ("dp", "seq", "head"))
    ratio = tok_rows * all_devices / count
    grad_tokens = (ratio * (cotangent + input_grad)).astype(jnp.bfloat16)
    return (
        grad_tokens,
        gain_total / count,
        ratio * combine_part,
        loss_total / (2.0 * feature * count),
    )


def solution(mesh):
    in_specs = (
        P(("dp", "seq", "head"), None),
        P(),
        P(("seq", "head"), None, None),
        P(("seq", "head"), None, None),
        P(("dp", "seq", "head"), None),
        P(("dp", "seq", "head"), None),
        P(("dp", "seq", "head")),
    )
    out_specs = (P(("dp", "seq", "head"), None), P(), P(("dp", "seq", "head"), None), P())
    return jax.shard_map(
        on_device, mesh=mesh, in_specs=in_specs, out_specs=out_specs, check_vma=False
    )
```

profile of v0, /device:TPU:1, one launch (start us, length us, event | category | flops | bytes accessed | tf_op | source)
XLA Modules:
  0.0 298.5 jit_solution(7343116769896336238)
XLA Ops:
  0.6 0.0 copy-start
  0.6 0.8 copy.27
  1.5 0.1 eq.46
  1.6 0.1 eq.50
  1.8 1.2 fusion.34
  2.9 0.6 reduce-window.6
  3.6 0.2 slice_reduce_fusion
  3.8 0.1 fusion.49
  3.9 0.1 reduce_sum.108
  4.1 0.1 copy.31
  4.1 0.1 fusion.45
  4.2 0.0 copy-done
  4.2 1.2 convolution_convert_fusion
  5.4 0.2 reshape.132
  5.5 36.6 %all_to_all.20 = bf16[64,4,1536]{2,1,0:T(4,128)(2,1)S(1)} all-to-all(bf16[64,4,1536]{2,1,0:T(4,128)(2,1)S(1)} %reshape.132), channel_id=1, replica_groups=mesh['dp'=12,'seq'=8,'head'=8] {'seq','head'}, dimensions={0} | all-to-all | bytes 1572864 | tf_op jit(solution)/shard_map/all_to_all | solution.py:10
  42.2 0.2 reshape.133
  42.3 3.7 %fusion.6 = f32[256,1536]{1,0:T(8,128)S(1)} fusion(bf16[256,1536]{1,0:T(8,128)(2,1)S(1)} %reshape.133, bf16[1,1536,1536]{2,1,0:T(8,128)(2,1)} %param.9), kind=kOutput, calls=%fused_computation.8 | convolution fusion | flops 1207959552 | bytes 7077888 | tf_op jit(solution)/shard_map/dot_general | solution.py:42
  46.1 0.0 copy-start.8
  46.1 1.1 copy-done.8
  47.2 3.8 %fusion.17 = bf16[256,1536]{1,0:T(8,128)(2,1)S(1)} fusion(bf16[1,1536,1536]{2,1,0:T(8,128)(2,1)} %param.10, f32[256,1536]{1,0:T(8,128)S(1)} %fusion.6), kind=kOutput, calls=%fused_computation.14 | convolution fusion | flops 1210712064 | bytes 7077888 | tf_op jit(solution)/shard_map/dot_general | solution.py:45
  51.0 0.0 copy-start.6
  51.0 0.0 copy-start.4
  51.0 1.1 reshape.134
  52.1 6.6 %all-to-all-start.1 = ((bf16[64,4,1536]{2,1,0:T(4,128)(2,1)}), bf16[64,4,1536]{2,1,0:T(4,128)(2,1)S(1)}, u32[]{:S(2)}, u32[]{:S(2)}) async-start(bf16[64,4,1536]{2,1,0:T(4,128)(2,1)} %reshape.134), calls=%async_computation.1 | async-start | bytes 1572864 | tf_op jit(solution)/shard_map/all_to_all | solution.py:10
  58.6 0.0 copy-done.6
  58.6 0.5 convert_element_type.63
  59.2 0.0 copy-done.4
  59.2 0.1 copy.26
  59.3 0.1 mul.169
  59.4 0.1 mul.164
  59.6 0.3 copy-done.1
  59.9 21.5 %all-to-all-done.1 = bf16[64,4,1536]{2,1,0:T(4,128)(2,1)S(1)} async-done(((bf16[64,4,1536]{2,1,0:T(4,128)(2,1)}), bf16[64,4,1536]{2,1,0:T(4,128)(2,1)S(1)}, u32[]{:S(2)}, u32[]{:S(2)}) %all-to-all-start.1) | async-done | bytes 786464 | tf_op jit(solution)/shard_map/all_to_all | solution.py:10
  81.4 0.2 reshape.135
  81.5 1.3 gather_fusion
  82.8 1.0 reshape.140
  83.8 0.0 copy-start.5
  83.8 3.1 %multiply_reduce_fusion.1 = f32[128,1536]{1,0:T(8,128)S(1)} fusion(f32[128,2,1536]{2,1,0:T(2,128)S(1)} %reshape.140, f32[128,2]{1,0:T(8,128)} %copy-done.1), kind=kLoop, calls=%fused_computation.18 | loop fusion | flops 589824 | bytes 2360320 | tf_op jit(solution)/shard_map/reduce_sum | solution.py:50
  86.9 0.0 copy-done.5
  86.9 0.1 fusion.40
  87.0 1.7 mul.171
  88.7 3.2 %mul.172 = f32[256,1536]{1,0:T(8,128)} reshape(f32[128,2,1536]{2,1,0:T(2,128)} %mul.171) | data formatting | bytes 3145728 | tf_op jit(solution)/shard_map/mul | solution.py:55
  91.8 2.7 convolution_convert_fusion.1
  94.6 2.4 reshape.136
  97.0 29.4 %all_to_all.21 = bf16[64,4,1536]{2,1,0:T(4,128)(2,1)} all-to-all(bf16[64,4,1536]{2,1,0:T(4,128)(2,1)} %reshape.136), channel_id=1, replica_groups=mesh['dp'=12,'seq'=8,'head'=8] {'seq','head'}, dimensions={0} | all-to-all | bytes 1572864 | tf_op jit(solution)/shard_map/all_to_all | solution.py:10
  126.4 2.3 reshape.137
  128.7 8.0 %fusion.14 = bf16[256,1536]{1,0:T(8,128)(2,1)} fusion(bf16[1,1536,1536]{2,1,0:T(8,128)(2,1)} %param.9, bf16[256,1536]{1,0:T(8,128)(2,1)} %reshape.137, bf16[1,1536,1536]{2,1,0:T(8,128)(2,1)} %param.10, f32[256,1536]{1,0:T(8,128)} %copy-done.8), kind=kOutput, calls=%fused_computation.13 | convolution fusion | flops 2420244480 | bytes 12582912 | tf_op jit(solution)/shard_map/dot_general | solution.py:68
  136.7 2.4 reshape.138
  139.1 6.9 %all-to-all-start.3 = ((bf16[64,4,1536]{2,1,0:T(4,128)(2,1)}), bf16[64,4,1536]{2,1,0:T(4,128)(2,1)}, u32[]{:S(2)}, u32[]{:S(2)}) async-start(bf16[64,4,1536]{2,1,0:T(4,128)(2,1)} %reshape.138), calls=%async_computation.3 | async-start | bytes 1572864 | tf_op jit(solution)/shard_map/all_to_all | solution.py:10
  146.0 1.4 multiply_reduce_fusion
  147.5 21.2 %all-to-all-done.3 = bf16[64,4,1536]{2,1,0:T(4,128)(2,1)} async-done(((bf16[64,4,1536]{2,1,0:T(4,128)(2,1)}), bf16[64,4,1536]{2,1,0:T(4,128)(2,1)}, u32[]{:S(2)}, u32[]{:S(2)}) %all-to-all-start.3) | async-done | bytes 786464 | tf_op jit(solution)/shard_map/all_to_all | solution.py:10
  168.7 1.6 reshape.139
  170.3 1.3 gather_fusion.1
  171.5 2.1 reshape.141
  173.7 3.3 %reduce_sum.113 = f32[128,1536]{1,0:T(8,128)S(1)} reduce(f32[128,2,1536]{2,1,0:T(2,128)} %reshape.141, f32[]{:T(128)} %constant.6.clone.1), dimensions={1}, to_apply=%region_8.9 | reduce | flops 196608 | bytes 2359300 | tf_op jit(solution)/shard_map/reduce_sum | solution.py:72
  176.9 0.0 copy-done.3
  177.0 0.0 copy-start.7
  177.0 0.4 fusion.33
  177.4 0.3 copy-done.7
  177.6 0.6 multiply_reduce_fusion.3
  178.2 114.1 %all-reduce = (f32[]{:T(128)}, f32[1536]{0:T(1024)S(1)}, f32[]{:T(128)}) all-reduce(f32[]{:T(128)} %get-tuple-element.16, f32[1536]{0:T(1024)S(1)} %get-tuple-element.12, f32[]{:T(128)} %get-tuple-element.15), channel_id=1, replica_groups=mesh['dp'=12,'seq'=8,'head'=8] {'dp','seq','head'}, use_global_device_ids=true, to_apply=%region_1.0 | all-reduce | flops 1538 | bytes 12304 | tf_op jit(solution)/shard_map/psum | solution.py:21
  293.7 1.1 fusion.32
  294.8 0.0 copy-done.2
  294.8 0.6 copy.33
  295.4 1.3 broadcast_divide_fusion
  (13 shorter events, 0.1 us)
Async XLA Ops:
  0.6 3.6 %copy-start = (bf16[128,1536]{1,0:T(8,128)(2,1)S(1)}, bf16[128,1536]{1,0:T(8,128)(2,1)}, u32[]{:S(2)}) copy-start(bf16[128,1536]{1,0:T(8,128)(2,1)} %param.7) | copy-start | bytes 1179652
  46.1 1.2 copy-start.8
  51.0 7.7 %copy-start.6 = (s32[128]{0:T(128)S(1)}, s32[128]{0:T(128)}, u32[]{:S(2)}) copy-start(s32[128]{0:T(128)} %param.13) | copy-start | bytes 1540
  51.0 8.2 %copy-start.4 = (f32[128,2]{0,1:T(2,128)S(1)}, f32[128,2]{0,1:T(2,128)}, u32[]{:S(2)}) copy-start(f32[128,2]{0,1:T(2,128)} %param.12) | copy-start | bytes 3076
  52.1 29.3 %all-to-all-start.1 = ((bf16[64,4,1536]{2,1,0:T(4,128)(2,1)}), bf16[64,4,1536]{2,1,0:T(4,128)(2,1)S(1)}, u32[]{:S(2)}, u32[]{:S(2)}) async-start(bf16[64,4,1536]{2,1,0:T(4,128)(2,1)} %reshape.134), calls=%async_computation.1 | async-start | bytes 1572864 | tf_op jit(solution)/shard_map/all_to_all | solution.py:10
  59.3 0.6 copy-start.1
  83.8 3.1 %copy-start.5 = (f32[128]{0:T(128)S(1)}, f32[128]{0:T(128)}, u32[]{:S(2)}) copy-start(f32[128]{0:T(128)} %convert_element_type.63) | copy-start | bytes 1540
  139.1 29.6 %all-to-all-start.3 = ((bf16[64,4,1536]{2,1,0:T(4,128)(2,1)}), bf16[64,4,1536]{2,1,0:T(4,128)(2,1)}, u32[]{:S(2)}, u32[]{:S(2)}) async-start(bf16[64,4,1536]{2,1,0:T(4,128)(2,1)} %reshape.138), calls=%async_computation.3 | async-start | bytes 1572864 | tf_op jit(solution)/shard_map/all_to_all | solution.py:10
  173.7 3.3 %copy-start.3 = (f32[1536]{0:T(1024)S(1)}, f32[1536]{0:T(1024)}, u32[]{:S(2)}) copy-start(f32[1536]{0:T(1024)} %param.8) | copy-start | bytes 18436
  177.0 0.7 copy-start.7
  177.3 117.4 %copy-start.2 = (f32[128,2]{1,0:T(8,128)S(1)}, f32[128,2]{1,0:T(8,128)}, u32[]{:S(2)}) copy-start(f32[128,2]{1,0:T(8,128)} %multiply_reduce_fusion) | copy-start | bytes 3076
where the time goes:
time: 299 us
  blocking collectives  180 us (60%)
  waiting for transfers between devices  42.7 us (14%)
  local copies, waits for them, and re-layouts  24.9 us (8%)
  matrix products  19.4 us (6%)
  other arithmetic  13.8 us (5%)
  starting transfers between devices  13.5 us (5%)
  between operations  4.11 us (1%)
    psum x1, blocking collectives, on_device(): count = lax.psum(jnp.sum(mask_f), ('dp', 'seq', 'head'))  114 us
    all_to_all x2, blocking collectives, shuffle(): lax.all_to_all(blocks, ('seq', 'head'), split_axis=0, concat_axis=0, tile...  66 us
    all_to_all x2, waiting for transfers between devices, shuffle(): lax.all_to_all(blocks, ('seq', 'head'), split_axis=0, concat_axis=0, tile...  42.7 us
    all_to_all x2, starting transfers between devices, shuffle(): lax.all_to_all(blocks, ('seq', 'head'), split_axis=0, concat_axis=0, tile...  13.5 us
    dot_general x1, matrix products, on_device(): lax.dot_general(pre_grad, weight_up, (((1,), (1,)), ((), ())), preferred_...  8.03 us
    reshape x4, local copies, waits for them, and re-layouts, shuffle(): blocks = row_block.reshape(peer_count, capacity, feature)  6.02 us
  transfers between devices with their start and end apart: 2, of which 2 were waited for; matrix products, arithmetic and copies ran while one was open for 1% of the time, Pallas kernels for 0%

commit v1 on v0

v1 whole, which is shorter than its diff:
```python
import jax
import jax.numpy as jnp
from jax import lax
from jax.experimental import pallas as pl
from jax.experimental.pallas import tpu as pltpu
from jax.sharding import PartitionSpec as P

F32, BF16, I32 = jnp.float32, jnp.bfloat16, jnp.int32
MESH = pl.DeviceIdType.MESH
CAP = 4
FOLD = 4
CHUNKS = 4
NT = (((1,), (1,)), ((), ()))


def dot(a, b):
    return jnp.dot(a, b, preferred_element_type=F32)


def iota(shape, dim):
    return lax.broadcasted_iota(I32, shape, dim)


def kernel(sizes, tok, gain, wup_hbm, wdown_hbm, routes, comb, mask,
           out_tok, out_gain, out_comb, out_loss,
           wup, wdown, snd, rcv, xs, slope, nat, sel, cot, stats, arz, ars, ary,
           send_sem, recv_sem, w_sem, red_send, red_recv):
    dp_n, seq_n, head_n = sizes
    rows, width = tok.shape
    peers = seq_n * head_n
    per = peers // CHUNKS
    msg = CAP * FOLD
    crow = per * msg
    cnat = per * CAP
    cols = width // FOLD
    slots = peers * CAP
    xn = seq_n // 2
    me_z = lax.axis_index("dp")
    me_s = lax.axis_index("seq")
    me_h = lax.axis_index("head")
    me_x, me_c = me_s // 2, me_s % 2

    def at_offset(g, i, sign):
        dc, dh = i % 2, i // 2
        dx = (g + dh) % xn
        x = (me_x + sign * dx + xn) % xn
        return {"seq": x * 2 + (me_c + dc) % 2, "head": (me_h + sign * dh + head_n) % head_n}

    load_up = pltpu.make_async_copy(wup_hbm.at[0], wup, w_sem.at[0])
    load_down = pltpu.make_async_copy(wdown_hbm.at[0], wdown, w_sem.at[1])
    load_up.start()
    load_down.start()

    barrier = pltpu.get_barrier_semaphore()

    def greet(j, _):
        pl.semaphore_signal(barrier, inc=1, device_id=at_offset(j // per, j % per, 1),
                            device_id_type=MESH)
        return _
    lax.fori_loop(1, peers, greet, 0)

    def greet_z(j, _):
        pl.semaphore_signal(barrier, inc=1, device_id={"dp": (me_z + j) % dp_n},
                            device_id_type=MESH)
        return _
    lax.fori_loop(1, dp_n, greet_z, 0)

    q, m = iota((crow, crow), 0), iota((crow, crow), 1)
    fold_m = (m == ((q // CAP) % FOLD) * cnat + (q // msg) * CAP + q % CAP).astype(BF16)
    back_m = (q == ((m // CAP) % FOLD) * cnat + (m // msg) * CAP + m % CAP).astype(BF16)

    def fold(block):
        stack = jnp.concatenate([block[:, c * cols:(c + 1) * cols] for c in range(FOLD)], axis=0)
        return dot(fold_m, stack).astype(BF16)

    def unfold(block):
        stack = dot(back_m, block).astype(BF16)
        return jnp.concatenate([stack[c * cnat:(c + 1) * cnat] for c in range(FOLD)], axis=1)

    def at(g, n):
        return pl.ds(pl.multiple_of(g * n, n), n)

    def start(phase, g, sign):
        def one(i, _):
            where = at(g * per + i, msg)
            pltpu.make_async_remote_copy(
                src_ref=snd.at[phase, where], dst_ref=rcv.at[phase, where],
                send_sem=send_sem.at[phase], recv_sem=recv_sem.at[phase, g],
                device_id=at_offset(g, i, sign), device_id_type=MESH).start()
            return _
        lax.fori_loop(1 if g == 0 else 0, per, one, 0)
        if g == 0:
            pltpu.make_async_copy(snd.at[phase, pl.ds(0, msg)], rcv.at[phase, pl.ds(0, msg)],
                                  recv_sem.at[phase, 0]).start()

    def arrived(phase, g):
        where = rcv.at[phase, at(g, crow)]
        pltpu.make_async_copy(where, where, recv_sem.at[phase, g]).wait()

    BR = 16

    def norm(b, _):
        r = at(b, BR)
        x = tok[r, :].astype(F32)
        inverse = lax.rsqrt(jnp.mean(x * x, axis=1, keepdims=True) + 1e-05)
        nat[r, :] = (x * inverse * gain[...]).astype(BF16)
        return _
    lax.fori_loop(0, rows // BR, norm, 0)

    eye = iota((rows, rows), 0) == iota((rows, rows), 1)
    lower = (iota((rows, rows), 0) > iota((rows, rows), 1)).astype(BF16)
    r0, r1 = routes[:, 0:1], routes[:, 1:2]
    lanes = iota((rows, peers), 1)
    hot0, hot1 = (lanes == r0).astype(F32), (lanes == r1).astype(F32)
    before = dot(lower, (hot0 + hot1).astype(BF16))

    def slot_of(r, hot):
        turn = jnp.sum(before * hot, axis=1, keepdims=True).astype(I32)
        s, h = r // head_n, r % head_n
        dx = (s // 2 - me_x + xn) % xn
        dc = (s % 2 + me_c) % 2
        dh = (h - me_h + head_n) % head_n
        g = (dx - dh + head_n) % xn
        return (g * per + dh * 2 + dc) * CAP + turn

    s0, s1 = slot_of(r0, hot0), slot_of(r1, hot1)

    def row_of(col):
        return jnp.sum(jnp.where(eye, col.astype(F32), 0.0), axis=0, keepdims=True)

    s0_row, s1_row = row_of(s0).astype(I32), row_of(s1).astype(I32)
    mask_col = jnp.sum(jnp.where(eye, mask[...].astype(F32), 0.0), axis=1, keepdims=True)
    slot_lanes = iota((rows, slots), 1)
    pick0 = (slot_lanes == s0).astype(BF16)
    pick1 = (slot_lanes == s1).astype(BF16)
    sel[0:rows, :] = pick0
    sel[rows:2 * rows, :] = pick1

    def place(g):
        target = iota((cnat, rows), 0) + g * cnat
        return (target == s0_row).astype(BF16), (target == s1_row).astype(BF16)

    for g in range(CHUNKS):
        a, b = place(g)
        block = dot(a + b, nat[0:rows, :]).astype(BF16)
        snd[0, g * crow:(g + 1) * crow, :] = fold(block)
        if g == 0:
            pl.semaphore_wait(barrier, peers - 1 + dp_n - 1)
        start(0, g, 1)

    load_up.wait()
    load_down.wait()
    tile = 512
    tiles = width // tile

    for g in range(CHUNKS):
        arrived(0, g)
        r = slice(g * cnat, (g + 1) * cnat)
        xs[r, :] = unfold(rcv[0, g * crow:(g + 1) * crow, :])

        def up(n, _):
            c = at(n, tile)
            projected = dot(xs[r, :], wup[:, c])
            gate = jax.nn.sigmoid(1.702 * projected)
            slope[r, c] = gate + 1.702 * projected * gate * (1.0 - gate)
            nat[0:cnat, c] = (projected * gate).astype(BF16)
            return _
        lax.fori_loop(0, tiles, up, 0)

        def down(n, _):
            c = at(n, tile)
            nat[cnat:2 * cnat, c] = dot(nat[0:cnat, :], wdown[:, c]).astype(BF16)
            return _
        lax.fori_loop(0, tiles, down, 0)
        snd[1, g * crow:(g + 1) * crow, :] = fold(nat[cnat:2 * cnat, :])
        start(1, g, -1)

    for g in range(CHUNKS):
        arrived(1, g)
        nat[g * cnat:(g + 1) * cnat, :] = unfold(rcv[1, g * crow:(g + 1) * crow, :])

    c0, c1 = comb[:, 0:1], comb[:, 1:2]

    loss = jnp.zeros((rows, 1), F32)
    part0 = jnp.zeros((rows, 1), F32)
    part1 = jnp.zeros((rows, 1), F32)
    for n in range(tiles):
        c = slice(n * tile, (n + 1) * tile)
        both = dot(sel[...], nat[:, c])
        p0, p1 = both[0:rows], both[rows:2 * rows]
        mixed = tok[:, c].astype(F32) + c0 * p0 + c1 * p1
        cotangent = mask_col * mixed
        cot[:, c] = cotangent
        loss = loss + jnp.sum(cotangent * mixed, axis=1, keepdims=True)
        part0 = part0 + jnp.sum(cotangent * p0, axis=1, keepdims=True)
        part1 = part1 + jnp.sum(cotangent * p1, axis=1, keepdims=True)
        nat[0:rows, c] = (c0 * cotangent).astype(BF16)
        nat[rows:2 * rows, c] = (c1 * cotangent).astype(BF16)

    for g in range(CHUNKS):
        a, b = place(g)
        block = dot(jnp.concatenate([a, b], axis=1), nat[...]).astype(BF16)
        snd[2, g * crow:(g + 1) * crow, :] = fold(block)
        start(2, g, 1)

    stats[...] = jnp.zeros_like(stats)
    stats[12:13, :] = jnp.broadcast_to(jnp.sum(loss, axis=0, keepdims=True), (1, 128))
    stats[13:14, :] = jnp.broadcast_to(jnp.sum(mask_col, axis=0, keepdims=True), (1, 128))

    gain_part = [jnp.zeros((1, tile), F32) for _ in range(tiles)]
    for g in range(CHUNKS):
        arrived(2, g)
        r = slice(g * cnat, (g + 1) * cnat)
        nat[0:cnat, :] = unfold(rcv[2, g * crow:(g + 1) * crow, :])

        def down_t(n, _):
            c = at(n, tile)
            hidden_grad = lax.dot_general(nat[0:cnat, :], wdown[c, :], NT,
                                          preferred_element_type=F32)
            nat[cnat:2 * cnat, c] = (hidden_grad * slope[r, c]).astype(BF16)
            return _
        lax.fori_loop(0, tiles, down_t, 0)
        for n in range(tiles):
            c = slice(n * tile, (n + 1) * tile)
            row_grad = lax.dot_general(nat[cnat:2 * cnat, :], wup[c, :], NT,
                                       preferred_element_type=F32).astype(BF16)
            gain_part[n] = gain_part[n] + jnp.sum(
                row_grad.astype(F32) * xs[r, c].astype(F32), axis=0, keepdims=True)
            nat[2 * cnat:3 * cnat, c] = row_grad
        snd[3, g * crow:(g + 1) * crow, :] = fold(nat[2 * cnat:3 * cnat, :])
        if g == CHUNKS - 1:
            for n in range(tiles):
                for k in range(tile // 128):
                    at_k = n * (tile // 128) + k
                    stats[at_k:at_k + 1, :] = (
                        gain_part[n][:, k * 128:(k + 1) * 128]
                        / gain[:, at_k * 128:(at_k + 1) * 128])
            reduce_start(0, dp_n, me_z, "dp", stats, arz, red_send, red_recv)
        start(3, g, -1)

    total = reduce_end(0, dp_n, arz, stats, red_send, red_recv)
    stats[...] = total
    reduce_start(1, seq_n, me_s, "seq", stats, ars, red_send, red_recv)
    total = reduce_end(1, seq_n, ars, stats, red_send, red_recv)
    stats[...] = total
    reduce_start(2, head_n, me_h, "head", stats, ary, red_send, red_recv)
    total = reduce_end(2, head_n, ary, stats, red_send, red_recv)
    stats[...] = total

    count = stats[13:14, 0:1]
    ratio = (rows * dp_n * peers) / count
    for k in range(width // 128):
        out_gain[:, k * 128:(k + 1) * 128] = stats[k:k + 1, :] / count
    out_loss[...] = stats[12:13, 0:1] / (2.0 * width * count)
    out_comb[:, 0:1] = ratio * part0
    out_comb[:, 1:2] = ratio * part1

    for g in range(CHUNKS):
        arrived(3, g)
        nat[g * cnat:(g + 1) * cnat, :] = unfold(rcv[3, g * crow:(g + 1) * crow, :])
    sel[0:rows, :] = sel[0:rows, :] + sel[rows:2 * rows, :]
    for n in range(tiles):
        c = slice(n * tile, (n + 1) * tile)
        slope[0:rows, c] = dot(sel[0:rows, :], nat[:, c])

    def last(b, _):
        r = at(b, BR)
        x = tok[r, :].astype(F32)
        inverse = lax.rsqrt(jnp.mean(x * x, axis=1, keepdims=True) + 1e-05)
        normed = x * inverse
        grad = slope[r, :] * gain[...]
        mean = jnp.mean(grad * normed, axis=1, keepdims=True)
        out_tok[r, :] = (ratio * (cot[r, :] + inverse * (grad - normed * mean))).astype(BF16)
        return _
    lax.fori_loop(0, rows // BR, last, 0)

    for phase in range(4):
        sent = snd.at[phase, pl.ds(msg, (peers - 1) * msg)]
        pltpu.make_async_copy(sent, sent, send_sem.at[phase]).wait()


def reduce_start(stage, n, me, axis, stats, parts, send_sem, recv_sem):
    parts[pl.ds(n, 1)] = stats[...][None]
    parts[pl.ds(me, 1)] = stats[...][None]

    def one(j, _):
        pltpu.make_async_remote_copy(
            src_ref=parts.at[pl.ds(n, 1)], dst_ref=parts.at[pl.ds(me, 1)],
            send_sem=send_sem.at[stage], recv_sem=recv_sem.at[stage],
            device_id={axis: (me + j) % n}, device_id_type=MESH).start()
        return _
    lax.fori_loop(1, n, one, 0)


def reduce_end(stage, n, parts, stats, send_sem, recv_sem):
    where = parts.at[pl.ds(0, n - 1)]
    pltpu.make_async_copy(where, where, recv_sem.at[stage]).wait()
    pltpu.make_async_copy(where, where, send_sem.at[stage]).wait()
    total = parts[0]
    for k in range(1, n):
        total = total + parts[k]
    return total


def solution(mesh):
    sizes = (mesh.shape["dp"], mesh.shape["seq"], mesh.shape["head"])

    def on_device(tokens, norm_gain, w_up, w_down, routes, combine, loss_mask):
        rows, width = tokens.shape
        peers = sizes[1] * sizes[2]
        slots = peers * CAP
        folded = (4, slots * FOLD, width // FOLD)
        vmem = pl.BlockSpec(memory_space=pltpu.VMEM)
        hbm = pl.BlockSpec(memory_space=pl.ANY)
        grad_tokens, grad_gain, grad_combine, loss = pl.pallas_call(
            lambda *refs: kernel(sizes, *refs),
            out_shape=(
                jax.ShapeDtypeStruct((rows, width), BF16),
                jax.ShapeDtypeStruct((1, width), F32),
                jax.ShapeDtypeStruct((rows, 2), F32),
                jax.ShapeDtypeStruct((1, 1), F32),
            ),
            in_specs=[vmem, vmem, hbm, hbm, vmem, vmem, vmem],
            out_specs=(vmem, vmem, vmem, vmem),
            scratch_shapes=[
                pltpu.VMEM(w_up.shape[1:], BF16),
                pltpu.VMEM(w_down.shape[1:], BF16),
                pltpu.VMEM(folded, BF16),
                pltpu.VMEM(folded, BF16),
                pltpu.VMEM((slots, width), BF16),
                pltpu.VMEM((slots, width), F32),
                pltpu.VMEM((slots, width), BF16),
                pltpu.VMEM((2 * rows, slots), BF16),
                pltpu.VMEM((rows, width), F32),
                pltpu.VMEM((16, 128), F32),
                pltpu.VMEM((sizes[0] + 1, 16, 128), F32),
                pltpu.VMEM((sizes[1] + 1, 16, 128), F32),
                pltpu.VMEM((sizes[2] + 1, 16, 128), F32),
                pltpu.SemaphoreType.DMA((4,)),
                pltpu.SemaphoreType.DMA((4, CHUNKS)),
                pltpu.SemaphoreType.DMA((2,)),
                pltpu.SemaphoreType.DMA((3,)),
                pltpu.SemaphoreType.DMA((3,)),
            ],
            compiler_params=pltpu.CompilerParams(
                collective_id=1, has_side_effects=True, vmem_limit_bytes=48 * 2**20),
            cost_estimate=pl.CostEstimate(
                flops=8 * slots * width * width, bytes_accessed=4 * width * width,
                transcendentals=slots * width),
            name="moe",
        )(tokens, norm_gain.reshape(1, width), w_up, w_down, routes, combine,
          loss_mask.reshape(1, rows))
        return grad_tokens, grad_gain.reshape(width), grad_combine, loss.reshape(())

    split = ("dp", "seq", "head")
    in_specs = (P(split, None), P(), P(("seq", "head"), None, None), P(("seq", "head"), None, None),
                P(split, None), P(split, None), P(split))
    out_specs = (P(split, None), P(), P(split, None), P())
    return jax.shard_map(on_device, mesh=mesh, in_specs=in_specs, out_specs=out_specs,
                         check_vma=False)
```

time: 299 us -> 118 us (0.39)
  blocking collectives: 180 us -> 0 us
  Pallas kernels: 0 us -> 107 us
  waiting for transfers between devices: 42.7 us -> 0 us
  matrix products: 19.4 us -> 0 us
  local copies, waits for them, and re-layouts: 24.9 us -> 7.64 us
  starting transfers between devices: 13.5 us -> 0 us
  other arithmetic: 13.8 us -> 0.62 us
    psum x1 -> x0, blocking collectives: 114 us -> none  [on_device(): count = lax.psum(jnp.sum(mask_f), ('dp', 'seq', 'head'))]
    pallas_call x0 -> x1, Pallas kernels: none -> 107 us  [on_device(): pl.pallas_call(lambda *refs: kernel(sizes, *refs), out_shape=(jax.ShapeDt...]
    all_to_all x2 -> x0, blocking collectives: 66 us -> none  [shuffle(): lax.all_to_all(blocks, ('seq', 'head'), split_axis=0, concat_axis=0, tile...]
    all_to_all x2 -> x0, waiting for transfers between devices: 42.7 us -> none  [shuffle(): lax.all_to_all(blocks, ('seq', 'head'), split_axis=0, concat_axis=0, tile...]
    dot_general x5 -> x0, matrix products: 19.4 us -> none  [the longest x1 8.03 us: on_device(): lax.dot_general(pre_grad, weight_up, (((1,), (1,)), ((), ())), preferred_...]
    all_to_all x2 -> x0, starting transfers between devices: 13.5 us -> none  [shuffle(): lax.all_to_all(blocks, ('seq', 'head'), split_axis=0, concat_axis=0, tile...]
    reduce_sum x8 -> x0, other arithmetic: 10.1 us -> none  [the longest x1 3.28 us: on_device(): jnp.sum(returned_grad[bucket].reshape(tok_rows, top_count, feature).astyp...]
    reshape x8 -> x1, local copies, waits for them, and re-layouts: 10.2 us -> 0.7 us  [on_device(): norm_gain.reshape(1, width)]
  transfers between devices with their start and end apart: 2 -> 0, of which waited for: 2 -> 0; matrix products, arithmetic and copies ran while one was open for 1% -> 0% of each run, Pallas kernels for 0% -> 0%
where the time goes in v1:
time: 118 us
  Pallas kernels  107 us (91%)
  local copies, waits for them, and re-layouts  7.64 us (6%)
  between operations  2.41 us (2%)
    pallas_call x1, Pallas kernels, on_device(): pl.pallas_call(lambda *refs: kernel(sizes, *refs), out_shape=(jax.ShapeDt...  107 us
    unnamed x10, local copies, waits for them, and re-layouts  6.93 us

profile of v1, /device:TPU:1, one launch (start us, length us, event | category | flops | bytes accessed | tf_op | source)
XLA Modules:
  0.0 117.8 jit_solution(17255536510722587999)
XLA Ops:
  0.6 0.7 reshape.20.refs_1_
  1.3 0.8 copy.11.refs_4_
  2.1 0.8 copy.12.refs_5_
  2.9 0.0 copy-start
  2.9 2.3 %copy-done = bf16[1,1536,1536]{2,1,0:T(8,128)(2,1)S(1)} copy-done((bf16[1,1536,1536]{2,1,0:T(8,128)(2,1)S(1)}, bf16[1,1536,1536]{2,1,0:T(8,128)(2,1)}, u32[]{:S(2)}) %copy-start) | copy-done | bytes 4718616
  5.2 0.0 copy-start.1
  5.2 1.0 copy-done.1
  6.2 0.0 copy-start.2
  6.2 0.7 copy-done.2
  6.9 107.2 %moe.1 = (bf16[128,1536]{1,0:T(8,128)(2,1)S(1)}, f32[1,1536]{1,0:T(1,128)S(1)}, f32[128,2]{1,0:T(8,128)S(1)}, f32[1,1]{1,0:T(1,128)}) custom-call(bf16[128,1536]{1,0:T(8,128)(2,1)S(1)} %copy-done.1, f32[1,1536]{1,0:T(1,128)S(1)} %reshape.20.refs_1_, bf16[1,1536,1536]{2,1,0:T(8,128)(2,1)S(1)} %copy-done, bf16[1,1536,1536]{2,1,0:T(8,128)(2,1)} %refs_3_.1, ...), custom_call_target="tpu_custom_call" | custom-call | flops 4831838208 | bytes 9437184 | tf_op jit(solution)/shard_map/moe/pallas_call | solution.py:315
  114.1 0.6 copy.13
  114.7 0.6 reduce
  115.3 0.7 copy.16
Async XLA Ops:
  2.9 2.3 %copy-start = (bf16[1,1536,1536]{2,1,0:T(8,128)(2,1)S(1)}, bf16[1,1536,1536]{2,1,0:T(8,128)(2,1)}, u32[]{:S(2)}) copy-start(bf16[1,1536,1536]{2,1,0:T(8,128)(2,1)} %refs_2_.1) | copy-start | bytes 14155780
  5.2 1.0 copy-start.1
  6.2 0.7 copy-start.2

commit v2 on v1

--- a/solution.py
+++ b/solution.py
@@ -21,10 +21,12 @@
     return lax.broadcasted_iota(I32, shape, dim)
 
 
-def kernel(sizes, tok, gain, wup_hbm, wdown_hbm, routes, comb, mask,
+def kernel(sizes, tok_hbm, gain_hbm, wup_hbm, wdown_hbm, routes_hbm, comb_hbm, mask_hbm,
            out_tok, out_gain, out_comb, out_loss,
-           wup, wdown, snd, rcv, xs, slope, nat, sel, cot, stats, arz, ars, ary,
-           send_sem, recv_sem, w_sem, red_send, red_recv):
+           tok, gain_v, routes, comb, mask, gain, inv,
+           wup, wdown, snd, rcv, xs, slope, nat, sel, cot, stats, arz, ars, ary, num, cz, cs, cy,
+           stats_all, num_all,
+           send_sem, recv_sem, w_sem, red_send, red_recv, go, mate_send, mate_recv):
     dp_n, seq_n, head_n = sizes
     rows, width = tok.shape
     peers = seq_n * head_n
@@ -46,24 +48,44 @@
         x = (me_x + sign * dx + xn) % xn
         return {"seq": x * 2 + (me_c + dc) % 2, "head": (me_h + sign * dh + head_n) % head_n}
 
-    load_up = pltpu.make_async_copy(wup_hbm.at[0], wup, w_sem.at[0])
-    load_down = pltpu.make_async_copy(wdown_hbm.at[0], wdown, w_sem.at[1])
-    load_up.start()
-    load_down.start()
+    pairs = ((routes_hbm, routes), (mask_hbm, mask), (comb_hbm, comb), (gain_hbm, gain_v),
+             (tok_hbm, tok), (wup_hbm.at[0], wup), (wdown_hbm.at[0], wdown))
+    loads = [pltpu.make_async_copy(a, b, w_sem.at[i]) for i, (a, b) in enumerate(pairs)]
+    for load in loads:
+        load.start()
 
     barrier = pltpu.get_barrier_semaphore()
 
     def greet(j, _):
-        pl.semaphore_signal(barrier, inc=1, device_id=at_offset(j // per, j % per, 1),
+        x, h = (me_x + j // head_n) % xn, (me_h + j % head_n) % head_n
+        pl.semaphore_signal(barrier, inc=1, device_id={"seq": x * 2 + 1, "head": h},
                             device_id_type=MESH)
         return _
-    lax.fori_loop(1, peers, greet, 0)
-
-    def greet_z(j, _):
-        pl.semaphore_signal(barrier, inc=1, device_id={"dp": (me_z + j) % dp_n},
-                            device_id_type=MESH)
-        return _
-    lax.fori_loop(1, dp_n, greet_z, 0)
+    lax.fori_loop(me_c, peers // 2, greet, 0)
+    mate = {"seq": me_x * 2 + 1 - me_c}
+
+    @pl.when(me_c == 0)
+    def _():
+        def greet_z(j, _):
+            pl.semaphore_signal(barrier, inc=1, device_id={"dp": (me_z + j) % dp_n},
+                                device_id_type=MESH)
+            return _
+        lax.fori_loop(1, dp_n, greet_z, 0)
+
+    def plane_ready():
+        @pl.when(me_c == 1)
+        def _():
+            pl.semaphore_wait(barrier, peers - 1)
+            pl.semaphore_signal(go, inc=1, device_id=mate, device_id_type=MESH)
+
+        @pl.when(me_c == 0)
+        def _():
+            pl.semaphore_wait(go, 1)
+
+    def to_mate(i, src, dst):
+        return pltpu.make_async_remote_copy(src_ref=src, dst_ref=dst, send_sem=mate_send.at[i],
+                                            recv_sem=mate_recv.at[i], device_id=mate,
+                                            device_id_type=MESH)
 
     q, m = iota((crow, crow), 0), iota((crow, crow), 1)
     fold_m = (m == ((q // CAP) % FOLD) * cnat + (q // msg) * CAP + q % CAP).astype(BF16)
@@ -99,23 +121,17 @@
 
     BR = 16
 
-    def norm(b, _):
-        r = at(b, BR)
-        x = tok[r, :].astype(F32)
-        inverse = lax.rsqrt(jnp.mean(x * x, axis=1, keepdims=True) + 1e-05)
-        nat[r, :] = (x * inverse * gain[...]).astype(BF16)
-        return _
-    lax.fori_loop(0, rows // BR, norm, 0)
-
+    for load in loads[:3]:
+        load.wait()
     eye = iota((rows, rows), 0) == iota((rows, rows), 1)
-    lower = (iota((rows, rows), 0) > iota((rows, rows), 1)).astype(BF16)
-    r0, r1 = routes[:, 0:1], routes[:, 1:2]
-    lanes = iota((rows, peers), 1)
-    hot0, hot1 = (lanes == r0).astype(F32), (lanes == r1).astype(F32)
-    before = dot(lower, (hot0 + hot1).astype(BF16))
+    earlier = (iota((rows, rows), 0) < iota((rows, rows), 1)).astype(BF16)
+    r0, r1 = routes[0:1, :], routes[1:2, :]
+    experts = iota((peers, rows), 0)
+    hot0, hot1 = (experts == r0).astype(F32), (experts == r1).astype(F32)
+    before = dot((hot0 + hot1).astype(BF16), earlier)
 
     def slot_of(r, hot):
-        turn = jnp.sum(before * hot, axis=1, keepdims=True).astype(I32)
+        turn = jnp.sum(before * hot, axis=0, keepdims=True).astype(I32)
         s, h = r // head_n, r % head_n
         dx = (s // 2 - me_x + xn) % xn
         dc = (s % 2 + me_c) % 2
@@ -123,13 +139,30 @@
         g = (dx - dh + head_n) % xn
         return (g * per + dh * 2 + dc) * CAP + turn
 
-    s0, s1 = slot_of(r0, hot0), slot_of(r1, hot1)
-
-    def row_of(col):
-        return jnp.sum(jnp.where(eye, col.astype(F32), 0.0), axis=0, keepdims=True)
-
-    s0_row, s1_row = row_of(s0).astype(I32), row_of(s1).astype(I32)
-    mask_col = jnp.sum(jnp.where(eye, mask[...].astype(F32), 0.0), axis=1, keepdims=True)
+    def col_of(row):
+        return jnp.sum(jnp.where(eye, row.astype(F32), 0.0), axis=1, keepdims=True)
+
+    def as_row(col):
+        return jnp.sum(jnp.where(eye, col, 0.0), axis=0, keepdims=True)
+
+    s0_row, s1_row = slot_of(r0, hot0), slot_of(r1, hot1)
+    s0, s1 = col_of(s0_row).astype(I32), col_of(s1_row).astype(I32)
+    mask_col = col_of(mask[...])
+
+    for load in loads[3:5]:
+        load.wait()
+    for k in range(width // 128):
+        gain[:, k * 128:(k + 1) * 128] = gain_v[k:k + 1, :]
+
+    def norm(b, _):
+        r = at(b, BR)
+        x = tok[r, :].astype(F32)
+        inverse = lax.rsqrt(jnp.mean(x * x, axis=1, keepdims=True) + 1e-05)
+        inv[r, :] = inverse
+        nat[r, :] = (x * inverse * gain[...]).astype(BF16)
+        return _
+    lax.fori_loop(0, rows // BR, norm, 0)
+
     slot_lanes = iota((rows, slots), 1)
     pick0 = (slot_lanes == s0).astype(BF16)
     pick1 = (slot_lanes == s1).astype(BF16)
@@ -145,11 +178,13 @@
         block = dot(a + b, nat[0:rows, :]).astype(BF16)
         snd[0, g * crow:(g + 1) * crow, :] = fold(block)
         if g == 0:
-            pl.semaphore_wait(barrier, peers - 1 + dp_n - 1)
+            plane_ready()
         start(0, g, 1)
 
-    load_up.wait()
-    load_down.wait()
+    num[...] = jnp.broadcast_to(jnp.sum(mask_col, axis=0, keepdims=True), (8, 128))
+    reduce_start(3, seq_n, me_s, "seq", num, cs, red_send, red_recv)
+    for load in loads[5:]:
+        load.wait()
     tile = 512
     tiles = width // tile
 
@@ -175,11 +210,14 @@
         snd[1, g * crow:(g + 1) * crow, :] = fold(nat[cnat:2 * cnat, :])
         start(1, g, -1)
 
+    num[...] = reduce_end(3, seq_n, cs, red_send, red_recv)
+    reduce_start(4, head_n, me_h, "head", num, cy, red_send, red_recv)
+
     for g in range(CHUNKS):
         arrived(1, g)
         nat[g * cnat:(g + 1) * cnat, :] = unfold(rcv[1, g * crow:(g + 1) * crow, :])
 
-    c0, c1 = comb[:, 0:1], comb[:, 1:2]
+    c0, c1 = col_of(comb[0:1, :]), col_of(comb[1:2, :])
 
     loss = jnp.zeros((rows, 1), F32)
     part0 = jnp.zeros((rows, 1), F32)
@@ -203,9 +241,15 @@
         snd[2, g * crow:(g + 1) * crow, :] = fold(block)
         start(2, g, 1)
 
+    num[...] = reduce_end(4, head_n, cy, red_send, red_recv)
+
+    @pl.when(me_c == 0)
+    def _():
+        pl.semaphore_wait(barrier, dp_n - 1)
+        reduce_start(5, dp_n, me_z, "dp", num, cz, red_send, red_recv)
+
     stats[...] = jnp.zeros_like(stats)
     stats[12:13, :] = jnp.broadcast_to(jnp.sum(loss, axis=0, keepdims=True), (1, 128))
-    stats[13:14, :] = jnp.broadcast_to(jnp.sum(mask_col, axis=0, keepdims=True), (1, 128))
 
     gain_part = [jnp.zeros((1, tile), F32) for _ in range(tiles)]
     for g in range(CHUNKS):
@@ -235,48 +279,68 @@
                     stats[at_k:at_k + 1, :] = (
                         gain_part[n][:, k * 128:(k + 1) * 128]
                         / gain[:, at_k * 128:(at_k + 1) * 128])
-            reduce_start(0, dp_n, me_z, "dp", stats, arz, red_send, red_recv)
+            reduce_start(0, seq_n, me_s, "seq", stats, ars, red_send, red_recv)
         start(3, g, -1)
 
-    total = reduce_end(0, dp_n, arz, stats, red_send, red_recv)
-    stats[...] = total
-    reduce_start(1, seq_n, me_s, "seq", stats, ars, red_send, red_recv)
-    total = reduce_end(1, seq_n, ars, stats, red_send, red_recv)
-    stats[...] = total
-    reduce_start(2, head_n, me_h, "head", stats, ary, red_send, red_recv)
-    total = reduce_end(2, head_n, ary, stats, red_send, red_recv)
-    stats[...] = total
-
-    count = stats[13:14, 0:1]
+    stats[...] = reduce_end(0, seq_n, ars, red_send, red_recv)
+    reduce_start(1, head_n, me_h, "head", stats, ary, red_send, red_recv)
+    stats[...] = reduce_end(1, head_n, ary, red_send, red_recv)
+
+    @pl.when(me_c == 0)
+    def _():
+        reduce_start(2, dp_n, me_z, "dp", stats, arz, red_send, red_recv)
+        num_all[...] = reduce_end(5, dp_n, cz, red_send, red_recv)
+        copy = to_mate(0, num_all, num_all)
+        copy.start()
+        copy.wait_send()
+
+    @pl.when(me_c == 1)
+    def _():
+        to_mate(0, num_all, num_all).wait_recv()
+
+    count = num_all[0:1, 0:1]
     ratio = (rows * dp_n * peers) / count
-    for k in range(width // 128):
-        out_gain[:, k * 128:(k + 1) * 128] = stats[k:k + 1, :] / count
-    out_loss[...] = stats[12:13, 0:1] / (2.0 * width * count)
-    out_comb[:, 0:1] = ratio * part0
-    out_comb[:, 1:2] = ratio * part1
+    out_comb[0:1, :] = ratio * as_row(part0)
+    out_comb[1:2, :] = ratio * as_row(part1)
+    sel[0:rows, :] = sel[0:rows, :] + sel[rows:2 * rows, :]
 
     for g in range(CHUNKS):
         arrived(3, g)
         nat[g * cnat:(g + 1) * cnat, :] = unfold(rcv[3, g * crow:(g + 1) * crow, :])
-    sel[0:rows, :] = sel[0:rows, :] + sel[rows:2 * rows, :]
     for n in range(tiles):
         c = slice(n * tile, (n + 1) * tile)
         slope[0:rows, c] = dot(sel[0:rows, :], nat[:, c])
 
     def last(b, _):
         r = at(b, BR)
-        x = tok[r, :].astype(F32)
-        inverse = lax.rsqrt(jnp.mean(x * x, axis=1, keepdims=True) + 1e-05)
-        normed = x * inverse
+        inverse = inv[r, :]
+        normed = tok[r, :].astype(F32) * inverse
         grad = slope[r, :] * gain[...]
         mean = jnp.mean(grad * normed, axis=1, keepdims=True)
-        out_tok[r, :] = (ratio * (cot[r, :] + inverse * (grad - normed * mean))).astype(BF16)
+        tok[r, :] = (ratio * (cot[r, :] + inverse * (grad - normed * mean))).astype(BF16)
         return _
     lax.fori_loop(0, rows // BR, last, 0)
+    leave = pltpu.make_async_copy(tok, out_tok, w_sem.at[7])
+    leave.start()
 
     for phase in range(4):
         sent = snd.at[phase, pl.ds(msg, (peers - 1) * msg)]
         pltpu.make_async_copy(sent, sent, send_sem.at[phase]).wait()
+
+    @pl.when(me_c == 0)
+    def _():
+        stats_all[...] = reduce_end(2, dp_n, arz, red_send, red_recv)
+        copy = to_mate(1, stats_all, stats_all)
+        copy.start()
+        copy.wait_send()
+
+    @pl.when(me_c == 1)
+    def _():
+        to_mate(1, stats_all, stats_all).wait_recv()
+
+    leave.wait()
+    out_gain[...] = stats_all[0:width // 128, :] / count
+    out_loss[...] = stats_all[12:13, 0:1] / (2.0 * width * count)
 
 
 def reduce_start(stage, n, me, axis, stats, parts, send_sem, recv_sem):
@@ -292,7 +356,7 @@
     lax.fori_loop(1, n, one, 0)
 
 
-def reduce_end(stage, n, parts, stats, send_sem, recv_sem):
+def reduce_end(stage, n, parts, send_sem, recv_sem):
     where = parts.at[pl.ds(0, n - 1)]
     pltpu.make_async_copy(where, where, recv_sem.at[stage]).wait()
     pltpu.make_async_copy(where, where, send_sem.at[stage]).wait()
@@ -311,18 +375,25 @@
         slots = peers * CAP
         folded = (4, slots * FOLD, width // FOLD)
         vmem = pl.BlockSpec(memory_space=pltpu.VMEM)
-        hbm = pl.BlockSpec(memory_space=pl.ANY)
+        hbm = pl.BlockSpec(memory_space=pltpu.HBM)
         grad_tokens, grad_gain, grad_combine, loss = pl.pallas_call(
             lambda *refs: kernel(sizes, *refs),
             out_shape=(
                 jax.ShapeDtypeStruct((rows, width), BF16),
-                jax.ShapeDtypeStruct((1, width), F32),
-                jax.ShapeDtypeStruct((rows, 2), F32),
+                jax.ShapeDtypeStruct((width // 128, 128), F32),
+                jax.ShapeDtypeStruct((2, rows), F32),
                 jax.ShapeDtypeStruct((1, 1), F32),
             ),
-            in_specs=[vmem, vmem, hbm, hbm, vmem, vmem, vmem],
-            out_specs=(vmem, vmem, vmem, vmem),
+            in_specs=[hbm] * 7,
+            out_specs=(hbm, vmem, vmem, vmem),
             scratch_shapes=[
+                pltpu.VMEM((rows, width), BF16),
+                pltpu.VMEM((width // 128, 128), F32),
+                pltpu.VMEM((2, rows), I32),
+                pltpu.VMEM((2, rows), F32),
+                pltpu.VMEM((1, rows), I32),
+                pltpu.VMEM((1, width), F32),
+                pltpu.VMEM((rows, 1), F32),
                 pltpu.VMEM(w_up.shape[1:], BF16),
                 pltpu.VMEM(w_down.shape[1:], BF16),
                 pltpu.VMEM(folded, BF16),
@@ -336,21 +407,30 @@
                 pltpu.VMEM((sizes[0] + 1, 16, 128), F32),
                 pltpu.VMEM((sizes[1] + 1, 16, 128), F32),
                 pltpu.VMEM((sizes[2] + 1, 16, 128), F32),
+                pltpu.VMEM((8, 128), F32),
+                pltpu.VMEM((sizes[0] + 1, 8, 128), F32),
+                pltpu.VMEM((sizes[1] + 1, 8, 128), F32),
+                pltpu.VMEM((sizes[2] + 1, 8, 128), F32),
+                pltpu.VMEM((16, 128), F32),
+                pltpu.VMEM((8, 128), F32),
                 pltpu.SemaphoreType.DMA((4,)),
                 pltpu.SemaphoreType.DMA((4, CHUNKS)),
+                pltpu.SemaphoreType.DMA((8,)),
+                pltpu.SemaphoreType.DMA((6,)),
+                pltpu.SemaphoreType.DMA((6,)),
+                pltpu.SemaphoreType.REGULAR,
                 pltpu.SemaphoreType.DMA((2,)),
-                pltpu.SemaphoreType.DMA((3,)),
-                pltpu.SemaphoreType.DMA((3,)),
+                pltpu.SemaphoreType.DMA((2,)),
             ],
             compiler_params=pltpu.CompilerParams(
-                collective_id=1, has_side_effects=True, vmem_limit_bytes=48 * 2**20),
+                collective_id=1, has_side_effects=True, vmem_limit_bytes=60 * 2**20),
             cost_estimate=pl.CostEstimate(
                 flops=8 * slots * width * width, bytes_accessed=4 * width * width,
                 transcendentals=slots * width),
             name="moe",
-        )(tokens, norm_gain.reshape(1, width), w_up, w_down, routes, combine,
+        )(tokens, norm_gain.reshape(width // 128, 128), w_up, w_down, routes.T, combine.T,
           loss_mask.reshape(1, rows))
-        return grad_tokens, grad_gain.reshape(width), grad_combine, loss.reshape(())
+        return grad_tokens, grad_gain.reshape(width), grad_combine.T, loss.reshape(())
 
     split = ("dp", "seq", "head")
     in_specs = (P(split, None), P(), P(("seq", "head"), None, None), P(("seq", "head"), None, None),

time: 118 us -> 112 us (0.949)
  local copies, waits for them, and re-layouts: 7.64 us -> 4.31 us
  Pallas kernels: 107 us -> 105 us
    unnamed x10 -> x3, local copies, waits for them, and re-layouts: 6.93 us -> 4.31 us
    pallas_call x1, Pallas kernels: 107 us -> 105 us  [on_device(): pl.pallas_call(lambda *refs: kernel(sizes, *refs), out_shape=(jax.ShapeDt...]
where the time goes in v2:
time: 112 us
  Pallas kernels  105 us (94%)
  local copies, waits for them, and re-layouts  4.31 us (4%)
  between operations  2.34 us (2%)
    pallas_call x1, Pallas kernels, on_device(): pl.pallas_call(lambda *refs: kernel(sizes, *refs), out_shape=(jax.ShapeDt...  105 us
    unnamed x3, local copies, waits for them, and re-layouts  4.31 us

profile of v2, /device:TPU:1, one launch (start us, length us, event | category | flops | bytes accessed | tf_op | source)
XLA Modules:
  0.0 112.1 jit_solution(16452626244259107947)
XLA Ops:
  0.6 105.4 %moe.1 = (bf16[128,1536]{1,0:T(8,128)(2,1)}, f32[12,128]{1,0:T(8,128)}, f32[2,128]{1,0:T(2,128)}, f32[1,1]{1,0:T(1,128)}) custom-call(bf16[128,1536]{1,0:T(8,128)(2,1)} %refs_0_.1, f32[12,128]{1,0:T(8,128)} %bitcast.9, bf16[1,1536,1536]{2,1,0:T(8,128)(2,1)} %refs_2_.1, bf16[1,1536,1536]{2,1,0:T(8,128)(2,1)} %refs_3_.1, s32[2,128]{1,0:T(2,128)} %bitcast.10, ...), custom_call_target="tpu_custom_call" | custom-call | flops 4831838208 | bytes 9437184 | tf_op jit(solution)/shard_map/moe/pallas_call | solution.py:379
  106.1 1.8 %copy.15 = bf16[128,1536]{1,0:T(8,128)(2,1)} copy(bf16[128,1536]{1,0:T(8,128)(2,1)} %get-tuple-element.16) | data formatting | bytes 786432
  107.8 1.3 %copy.16 = f32[1536]{0:T(1024)} copy(f32[1536]{0:T(1024)} %bitcast.7) | data formatting | bytes 12288
  109.1 1.2 %copy.17 = f32[128,2]{0,1:T(2,128)} copy(f32[128,2]{0,1:T(2,128)} %bitcast.8) | data formatting | bytes 2048

commit v3 on v2

--- a/solution.py
+++ b/solution.py
@@ -10,6 +10,7 @@
 CAP = 4
 FOLD = 4
 CHUNKS = 4
+HELD = 2
 NT = (((1,), (1,)), ((), ()))
 
 
@@ -280,10 +281,13 @@
                         gain_part[n][:, k * 128:(k + 1) * 128]
                         / gain[:, at_k * 128:(at_k + 1) * 128])
             reduce_start(0, seq_n, me_s, "seq", stats, ars, red_send, red_recv)
-        start(3, g, -1)
+        if g < CHUNKS - HELD:
+            start(3, g, -1)
 
     stats[...] = reduce_end(0, seq_n, ars, red_send, red_recv)
     reduce_start(1, head_n, me_h, "head", stats, ary, red_send, red_recv)
+    for g in range(CHUNKS - HELD, CHUNKS):
+        start(3, g, -1)
     stats[...] = reduce_end(1, head_n, ary, red_send, red_recv)
 
     @pl.when(me_c == 0)
@@ -317,11 +321,9 @@
         normed = tok[r, :].astype(F32) * inverse
         grad = slope[r, :] * gain[...]
         mean = jnp.mean(grad * normed, axis=1, keepdims=True)
-        tok[r, :] = (ratio * (cot[r, :] + inverse * (grad - normed * mean))).astype(BF16)
+        out_tok[r, :] = (ratio * (cot[r, :] + inverse * (grad - normed * mean))).astype(BF16)
         return _
     lax.fori_loop(0, rows // BR, last, 0)
-    leave = pltpu.make_async_copy(tok, out_tok, w_sem.at[7])
-    leave.start()
 
     for phase in range(4):
         sent = snd.at[phase, pl.ds(msg, (peers - 1) * msg)]
@@ -338,7 +340,6 @@
     def _():
         to_mate(1, stats_all, stats_all).wait_recv()
 
-    leave.wait()
     out_gain[...] = stats_all[0:width // 128, :] / count
     out_loss[...] = stats_all[12:13, 0:1] / (2.0 * width * count)
 
@@ -376,6 +377,7 @@
         folded = (4, slots * FOLD, width // FOLD)
         vmem = pl.BlockSpec(memory_space=pltpu.VMEM)
         hbm = pl.BlockSpec(memory_space=pltpu.HBM)
+        keep = lambda x: pltpu.with_memory_space_constraint(x, pltpu.HBM)
         grad_tokens, grad_gain, grad_combine, loss = pl.pallas_call(
             lambda *refs: kernel(sizes, *refs),
             out_shape=(
@@ -385,7 +387,7 @@
                 jax.ShapeDtypeStruct((1, 1), F32),
             ),
             in_specs=[hbm] * 7,
-            out_specs=(hbm, vmem, vmem, vmem),
+            out_specs=(vmem, vmem, vmem, vmem),
             scratch_shapes=[
                 pltpu.VMEM((rows, width), BF16),
                 pltpu.VMEM((width // 128, 128), F32),
@@ -423,13 +425,13 @@
                 pltpu.SemaphoreType.DMA((2,)),
             ],
             compiler_params=pltpu.CompilerParams(
-                collective_id=1, has_side_effects=True, vmem_limit_bytes=60 * 2**20),
+                collective_id=1, has_side_effects=True, vmem_limit_bytes=48 * 2**20),
             cost_estimate=pl.CostEstimate(
                 flops=8 * slots * width * width, bytes_accessed=4 * width * width,
                 transcendentals=slots * width),
             name="moe",
-        )(tokens, norm_gain.reshape(width // 128, 128), w_up, w_down, routes.T, combine.T,
-          loss_mask.reshape(1, rows))
+        )(*map(keep, (tokens, norm_gain.reshape(width // 128, 128), w_up, w_down, routes.T,
+                      combine.T, loss_mask.reshape(1, rows))))
         return grad_tokens, grad_gain.reshape(width), grad_combine.T, loss.reshape(())
 
     split = ("dp", "seq", "head")

time: 112 us -> 107 us (0.955)
  Pallas kernels: 105 us -> 102 us
  local copies, waits for them, and re-layouts: 4.31 us -> 1.91 us
    pallas_call x1, Pallas kernels: 105 us -> 102 us  [on_device(): pl.pallas_call(lambda *refs: kernel(sizes, *refs), out_shape=(jax.ShapeDt...]
    unnamed x3, local copies, waits for them, and re-layouts: 4.31 us -> 1.91 us
where the time goes in v3:
time: 107 us
  Pallas kernels  102 us (95%)
  between operations  2.33 us (2%)
  local copies, waits for them, and re-layouts  1.91 us (2%)
    pallas_call x1, Pallas kernels, on_device(): pl.pallas_call(lambda *refs: kernel(sizes, *refs), out_shape=(jax.ShapeDt...  102 us

profile of v3, /device:TPU:1, one launch (start us, length us, event | category | flops | bytes accessed | tf_op | source)
XLA Modules:
  0.0 106.6 jit_solution(6978769248942774653)
XLA Ops:
  0.6 102.4 %moe.1 = (bf16[128,1536]{1,0:T(8,128)(2,1)S(1)}, f32[12,128]{1,0:T(8,128)S(1)}, f32[2,128]{1,0:T(2,128)S(1)}, f32[1,1]{1,0:T(1,128)}) custom-call(bf16[128,1536]{1,0:T(8,128)(2,1)} %refs_0_.1, f32[12,128]{1,0:T(8,128)} %bitcast.9, bf16[1,1536,1536]{2,1,0:T(8,128)(2,1)} %refs_2_.1, bf16[1,1536,1536]{2,1,0:T(8,128)(2,1)} %refs_3_.1, s32[2,128]{1,0:T(2,128)} %bitcast.10, ...), custom_call_target="tpu_custom_call" | custom-call | flops 4831838208 | bytes 9437184 | tf_op jit(solution)/shard_map/moe/pallas_call | solution.py:381
  103.0 0.7 copy.15
  103.8 0.6 copy.16
  104.4 0.6 copy.17

commit v4 on v3

--- a/solution.py
+++ b/solution.py
@@ -11,7 +11,6 @@
 FOLD = 4
 CHUNKS = 4
 HELD = 2
-NT = (((1,), (1,)), ((), ()))
 
 
 def dot(a, b):
@@ -25,7 +24,7 @@
 def kernel(sizes, tok_hbm, gain_hbm, wup_hbm, wdown_hbm, routes_hbm, comb_hbm, mask_hbm,
            out_tok, out_gain, out_comb, out_loss,
            tok, gain_v, routes, comb, mask, gain, inv,
-           wup, wdown, snd, rcv, xs, slope, nat, sel, cot, stats, arz, ars, ary, num, cz, cs, cy,
+           wup, wdown, wup_t, wdown_t, snd, rcv, xs, slope, nat, sel, cot, stats, arz, ars, ary, num, cz, cs, cy,
            stats_all, num_all,
            send_sem, recv_sem, w_sem, red_send, red_recv, go, mate_send, mate_recv):
     dp_n, seq_n, head_n = sizes
@@ -65,14 +64,6 @@
     lax.fori_loop(me_c, peers // 2, greet, 0)
     mate = {"seq": me_x * 2 + 1 - me_c}
 
-    @pl.when(me_c == 0)
-    def _():
-        def greet_z(j, _):
-            pl.semaphore_signal(barrier, inc=1, device_id={"dp": (me_z + j) % dp_n},
-                                device_id_type=MESH)
-            return _
-        lax.fori_loop(1, dp_n, greet_z, 0)
-
     def plane_ready():
         @pl.when(me_c == 1)
         def _():
@@ -182,12 +173,29 @@
             plane_ready()
         start(0, g, 1)
 
+    @pl.when(me_c == 0)
+    def _():
+        def greet_z(j, _):
+            pl.semaphore_signal(barrier, inc=1, device_id={"dp": (me_z + j) % dp_n},
+                                device_id_type=MESH)
+            return _
+        lax.fori_loop(1, dp_n, greet_z, 0)
+
     num[...] = jnp.broadcast_to(jnp.sum(mask_col, axis=0, keepdims=True), (8, 128))
     reduce_start(3, seq_n, me_s, "seq", num, cs, red_send, red_recv)
     for load in loads[5:]:
         load.wait()
-    tile = 512
+    tile = 768
     tiles = width // tile
+    edge = 256
+    blocks = width // edge
+
+    def turn(i, _):
+        a, b = at(i // blocks, edge), at(i % blocks, edge)
+        wdown_t[b, a] = wdown[a, b].T
+        wup_t[b, a] = wup[a, b].T
+        return _
+    lax.fori_loop(0, blocks * blocks, turn, 0)
 
     for g in range(CHUNKS):
         arrived(0, g)
@@ -223,8 +231,8 @@
     loss = jnp.zeros((rows, 1), F32)
     part0 = jnp.zeros((rows, 1), F32)
     part1 = jnp.zeros((rows, 1), F32)
-    for n in range(tiles):
-        c = slice(n * tile, (n + 1) * tile)
+    for n in range(width // 512):
+        c = slice(n * 512, (n + 1) * 512)
         both = dot(sel[...], nat[:, c])
         p0, p1 = both[0:rows], both[rows:2 * rows]
         mixed = tok[:, c].astype(F32) + c0 * p0 + c1 * p1
@@ -260,15 +268,13 @@
 
         def down_t(n, _):
             c = at(n, tile)
-            hidden_grad = lax.dot_general(nat[0:cnat, :], wdown[c, :], NT,
-                                          preferred_element_type=F32)
+            hidden_grad = dot(nat[0:cnat, :], wdown_t[:, c])
             nat[cnat:2 * cnat, c] = (hidden_grad * slope[r, c]).astype(BF16)
             return _
         lax.fori_loop(0, tiles, down_t, 0)
         for n in range(tiles):
             c = slice(n * tile, (n + 1) * tile)
-            row_grad = lax.dot_general(nat[cnat:2 * cnat, :], wup[c, :], NT,
-                                       preferred_element_type=F32).astype(BF16)
+            row_grad = dot(nat[cnat:2 * cnat, :], wup_t[:, c]).astype(BF16)
             gain_part[n] = gain_part[n] + jnp.sum(
                 row_grad.astype(F32) * xs[r, c].astype(F32), axis=0, keepdims=True)
             nat[2 * cnat:3 * cnat, c] = row_grad
@@ -311,8 +317,8 @@
     for g in range(CHUNKS):
         arrived(3, g)
         nat[g * cnat:(g + 1) * cnat, :] = unfold(rcv[3, g * crow:(g + 1) * crow, :])
-    for n in range(tiles):
-        c = slice(n * tile, (n + 1) * tile)
+    for n in range(width // 512):
+        c = slice(n * 512, (n + 1) * 512)
         slope[0:rows, c] = dot(sel[0:rows, :], nat[:, c])
 
     def last(b, _):
@@ -396,6 +402,8 @@
                 pltpu.VMEM((1, rows), I32),
                 pltpu.VMEM((1, width), F32),
                 pltpu.VMEM((rows, 1), F32),
+                pltpu.VMEM(w_up.shape[1:], BF16),
+                pltpu.VMEM(w_down.shape[1:], BF16),
                 pltpu.VMEM(w_up.shape[1:], BF16),
                 pltpu.VMEM(w_down.shape[1:], BF16),
                 pltpu.VMEM(folded, BF16),

time: 107 us -> 106 us (level)
    pallas_call x1, Pallas kernels: 102 us -> 101 us  [on_device(): pl.pallas_call(lambda *refs: kernel(sizes, *refs), out_shape=(jax.ShapeDt...]
where the time goes in v4:
time: 106 us
  Pallas kernels  101 us (95%)
  between operations  2.33 us (2%)
  local copies, waits for them, and re-layouts  1.91 us (2%)
    pallas_call x1, Pallas kernels, on_device(): pl.pallas_call(lambda *refs: kernel(sizes, *refs), out_shape=(jax.ShapeDt...  101 us

profile of v4, /device:TPU:1, one launch (start us, length us, event | category | flops | bytes accessed | tf_op | source)
XLA Modules:
  0.0 105.6 jit_solution(12410316548967400424)
XLA Ops:
  0.6 101.3 %moe.1 = (bf16[128,1536]{1,0:T(8,128)(2,1)S(1)}, f32[12,128]{1,0:T(8,128)S(1)}, f32[2,128]{1,0:T(2,128)S(1)}, f32[1,1]{1,0:T(1,128)}) custom-call(bf16[128,1536]{1,0:T(8,128)(2,1)} %refs_0_.1, f32[12,128]{1,0:T(8,128)} %bitcast.9, bf16[1,1536,1536]{2,1,0:T(8,128)(2,1)} %refs_2_.1, bf16[1,1536,1536]{2,1,0:T(8,128)(2,1)} %refs_3_.1, s32[2,128]{1,0:T(2,128)} %bitcast.10, ...), custom_call_target="tpu_custom_call" | custom-call | flops 4831838208 | bytes 9437184 | tf_op jit(solution)/shard_map/moe/pallas_call | solution.py:387
  102.0 0.7 copy.15
  102.7 0.6 copy.16
  103.3 0.6 copy.17

commit v5 on v4

--- a/solution.py
+++ b/solution.py
@@ -10,7 +10,6 @@
 CAP = 4
 FOLD = 4
 CHUNKS = 4
-HELD = 2
 
 
 def dot(a, b):
@@ -111,7 +110,7 @@
         where = rcv.at[phase, at(g, crow)]
         pltpu.make_async_copy(where, where, recv_sem.at[phase, g]).wait()
 
-    BR = 16
+    BR = 32
 
     for load in loads[:3]:
         load.wait()
@@ -278,7 +277,6 @@
             gain_part[n] = gain_part[n] + jnp.sum(
                 row_grad.astype(F32) * xs[r, c].astype(F32), axis=0, keepdims=True)
             nat[2 * cnat:3 * cnat, c] = row_grad
-        snd[3, g * crow:(g + 1) * crow, :] = fold(nat[2 * cnat:3 * cnat, :])
         if g == CHUNKS - 1:
             for n in range(tiles):
                 for k in range(tile // 128):
@@ -287,13 +285,14 @@
                         gain_part[n][:, k * 128:(k + 1) * 128]
                         / gain[:, at_k * 128:(at_k + 1) * 128])
             reduce_start(0, seq_n, me_s, "seq", stats, ars, red_send, red_recv)
-        if g < CHUNKS - HELD:
+            start(3, g - 1, -1)
+        snd[3, g * crow:(g + 1) * crow, :] = fold(nat[2 * cnat:3 * cnat, :])
+        if g < CHUNKS - 2:
             start(3, g, -1)
 
     stats[...] = reduce_end(0, seq_n, ars, red_send, red_recv)
     reduce_start(1, head_n, me_h, "head", stats, ary, red_send, red_recv)
-    for g in range(CHUNKS - HELD, CHUNKS):
-        start(3, g, -1)
+    start(3, CHUNKS - 1, -1)
     stats[...] = reduce_end(1, head_n, ary, red_send, red_recv)
 
     @pl.when(me_c == 0)

time: 106 us -> 107 us (level)
  Pallas kernels: 101 us -> 103 us
    pallas_call x1, Pallas kernels: 101 us -> 103 us  [on_device(): pl.pallas_call(lambda *refs: kernel(sizes, *refs), out_shape=(jax.ShapeDt...]
where the time goes in v5:
time: 107 us
  Pallas kernels  103 us (96%)
  between operations  2.33 us (2%)
  local copies, waits for them, and re-layouts  1.91 us (2%)
    pallas_call x1, Pallas kernels, on_device(): pl.pallas_call(lambda *refs: kernel(sizes, *refs), out_shape=(jax.ShapeDt...  103 us

profile of v5, /device:TPU:1, one launch (start us, length us, event | category | flops | bytes accessed | tf_op | source)
XLA Modules:
  0.0 107.1 jit_solution(14188643308467266293)
XLA Ops:
  0.6 102.9 %moe.1 = (bf16[128,1536]{1,0:T(8,128)(2,1)S(1)}, f32[12,128]{1,0:T(8,128)S(1)}, f32[2,128]{1,0:T(2,128)S(1)}, f32[1,1]{1,0:T(1,128)}) custom-call(bf16[128,1536]{1,0:T(8,128)(2,1)} %refs_0_.1, f32[12,128]{1,0:T(8,128)} %bitcast.9, bf16[1,1536,1536]{2,1,0:T(8,128)(2,1)} %refs_2_.1, bf16[1,1536,1536]{2,1,0:T(8,128)(2,1)} %refs_3_.1, s32[2,128]{1,0:T(2,128)} %bitcast.10, ...), custom_call_target="tpu_custom_call" | custom-call | flops 4831838208 | bytes 9437184 | tf_op jit(solution)/shard_map/moe/pallas_call | solution.py:386
  103.5 0.7 copy.15
  104.3 0.6 copy.16
  104.9 0.6 copy.17

commit v6 on v4

--- a/solution.py
+++ b/solution.py
@@ -111,7 +111,7 @@
         where = rcv.at[phase, at(g, crow)]
         pltpu.make_async_copy(where, where, recv_sem.at[phase, g]).wait()
 
-    BR = 16
+    BR = 32
 
     for load in loads[:3]:
         load.wait()
@@ -278,7 +278,6 @@
             gain_part[n] = gain_part[n] + jnp.sum(
                 row_grad.astype(F32) * xs[r, c].astype(F32), axis=0, keepdims=True)
             nat[2 * cnat:3 * cnat, c] = row_grad
-        snd[3, g * crow:(g + 1) * crow, :] = fold(nat[2 * cnat:3 * cnat, :])
         if g == CHUNKS - 1:
             for n in range(tiles):
                 for k in range(tile // 128):
@@ -287,6 +286,7 @@
                         gain_part[n][:, k * 128:(k + 1) * 128]
                         / gain[:, at_k * 128:(at_k + 1) * 128])
             reduce_start(0, seq_n, me_s, "seq", stats, ars, red_send, red_recv)
+        snd[3, g * crow:(g + 1) * crow, :] = fold(nat[2 * cnat:3 * cnat, :])
         if g < CHUNKS - HELD:
             start(3, g, -1)
 

time: 106 us -> 105 us (level)
  no operation moved by 1% of the time
where the time goes in v6:
time: 105 us
  Pallas kernels  101 us (96%)
  between operations  2.33 us (2%)
  local copies, waits for them, and re-layouts  1.91 us (2%)
    pallas_call x1, Pallas kernels, on_device(): pl.pallas_call(lambda *refs: kernel(sizes, *refs), out_shape=(jax.ShapeDt...  101 us

profile of v6, /device:TPU:1, one launch (start us, length us, event | category | flops | bytes accessed | tf_op | source)
XLA Modules:
  0.0 105.3 jit_solution(10019947008092327475)
XLA Ops:
  0.6 101.0 %moe.1 = (bf16[128,1536]{1,0:T(8,128)(2,1)S(1)}, f32[12,128]{1,0:T(8,128)S(1)}, f32[2,128]{1,0:T(2,128)S(1)}, f32[1,1]{1,0:T(1,128)}) custom-call(bf16[128,1536]{1,0:T(8,128)(2,1)} %refs_0_.1, f32[12,128]{1,0:T(8,128)} %bitcast.9, bf16[1,1536,1536]{2,1,0:T(8,128)(2,1)} %refs_2_.1, bf16[1,1536,1536]{2,1,0:T(8,128)(2,1)} %refs_3_.1, s32[2,128]{1,0:T(2,128)} %bitcast.10, ...), custom_call_target="tpu_custom_call" | custom-call | flops 4831838208 | bytes 9437184 | tf_op jit(solution)/shard_map/moe/pallas_call | solution.py:387
  101.7 0.7 copy.15
  102.4 0.6 copy.16
  103.0 0.6 copy.17
